TPU v7x, 32 devices: a whole 2x2x4 slice. The times are simulated.
32 devices in a mesh: strip: 8 (over z, y), sub: 4 (over x, core).
Axes of the slice: x: 2, y: 2, z: 4, core: 2. Of those that a mesh axis runs over, the one named last changes fastest.
Arguments:
- flow_field: bfloat16 [64, 512, 512], P('strip', None, 'sub'), may hold values from -6 to 6
- wall_source: bfloat16 [64, 512, 512], P('strip', None, 'sub'), may hold values from -1.1953125 to 1.1953125
- strip_rate: float32 [64], P('strip'), may hold values from 0.05 to 0.24
- strip_pos: int32 [64], P('strip'), may hold values from 0 to 63, as said below
- displace: float32 [64, 512], P('strip', 'sub'), may hold values from -6 to 6
- displace_prev: float32 [64, 512], P('strip', 'sub'), may hold values from -6 to 6
- tension_base: float32 [8], P('strip'), may hold values from 0.05 to 0.25
- anchor_seg: int32 [8], P('strip'), may hold values from 0 to 31
- seg_slot: int32 [32], replicated, may hold values from 0 to 31, each once
Outputs:
- flow_out: bfloat16 [64, 512, 512], P('strip', None, 'sub')
- displace_new: float32 [64, 512], P('strip', 'sub')
- deck_load: float32 [32, 512], P('strip', 'sub')
Inputs may be any that keep to these rules, and one draw needn't show every extreme that they name: `strip_pos`: a permutation of the 64 positions; the strips of one index of strip that belong to cables of one owner (position // 8) number 0 or exactly 2.
All inputs are finite; a program needn't handle non-finite values.
Results may differ from a plain program's by a relative error of at most 0.001.
Values may be sent and summed in bfloat16 or wider, within the bound.
A program may use at most 64 MiB of HBM per device.

v0:
```python
import math

import jax
import jax.numpy as jnp
from jax import lax
from jax.sharding import PartitionSpec as P

SWEEPS = 8


def padded(block, sides, width):
    for axis, dim in sides:
        count = lax.axis_size(axis)
        forward = [(i, i + 1) for i in range(count - 1)]
        backward = [(target, source) for source, target in forward]
        low = lax.ppermute(
            lax.slice_in_dim(block, block.shape[dim] - width, None, axis=dim), axis, forward
        )
        high = lax.ppermute(lax.slice_in_dim(block, 0, width, axis=dim), axis, backward)
        block = jnp.concatenate([low, block, high], axis=dim)
    return block


def relax_edge(extended, source_cells, rate_cells):
    interior = extended[:, :, 1:-1]
    row_padded = jnp.pad(interior, ((0, 0), (1, 1), (0, 0)))
    laplace = (
        row_padded[:, 2:]
        + row_padded[:, :-2]
        + extended[:, :, 2:]
        + extended[:, :, :-2]
        - 4.0 * interior
    )
    return interior + rate_cells * laplace + source_cells


def cable_update(positions, previous, force_cells, tension_base):
    extended = jnp.pad(positions, ((0, 0), (1, 1), (0, 0)))
    slopes = extended[:, 1:] - extended[:, :-1]
    stretch = jnp.mean(slopes * slopes, axis=1)
    tension = tension_base[:, None] * (1.0 + stretch)
    bending = extended[:, 2:] - 2.0 * positions + extended[:, :-2]
    moved = 2.0 * positions - previous + tension[:, None, :] * bending + 0.5 * force_cells
    return (moved, tension * moved[:, 0, :])


def per_device(
    flow_field,
    wall_source,
    strip_rate,
    strip_pos,
    displace,
    displace_prev,
    tension_base,
    anchor_seg,
    seg_slot,
):
    strip_total = flow_field.shape[0]
    grid_rows = flow_field.shape[1]
    slab_width = flow_field.shape[2]
    strip_count = lax.axis_size("strip")
    rate_cells = strip_rate[:, None, None]
    values = flow_field.astype(jnp.float32)
    source_cells = wall_source.astype(jnp.float32)
    for sweep_index in range(SWEEPS):
        extended = padded(values, (("sub", 2),), 1)
        values = relax_edge(extended, source_cells, rate_cells)
    flow_out = values.astype(jnp.bfloat16)
    force_rows = (jnp.sum(values, axis=1) * (1.0 / math.sqrt(grid_rows))).astype(jnp.bfloat16)
    capacity = max(2, 2 * strip_total // strip_count)
    owner_of = strip_pos // strip_total
    same_owner = owner_of[:, None] == owner_of[None, :]
    earlier = jnp.arange(strip_total)[None, :] < jnp.arange(strip_total)[:, None]
    order_in = jnp.sum((same_owner & earlier).astype(jnp.int32), axis=1)
    slot_index = owner_of * capacity + order_in
    packing = slot_index[None, :] == jnp.arange(strip_count * capacity, dtype=jnp.int32)[:, None]
    packed_rows = jnp.dot(
        packing.astype(jnp.bfloat16), force_rows, preferred_element_type=jnp.float32
    ).astype(jnp.bfloat16)
    packed_pos = jnp.where(
        jnp.any(packing, axis=1), jnp.sum(jnp.where(packing, strip_pos[None, :], 0), axis=1), -1
    )
    sent_rows, sent_pos = (
        lax.all_to_all(
            packed_rows.reshape(strip_count, capacity, slab_width),
            "strip",
            split_axis=0,
            concat_axis=0,
            tiled=True,
        ),
        lax.all_to_all(
            packed_pos.reshape(strip_count, capacity),
            "strip",
            split_axis=0,
            concat_axis=0,
            tiled=True,
        ),
    )
    local_pos = sent_pos.reshape(-1) - lax.axis_index("strip") * strip_total
    placing = jnp.arange(strip_total, dtype=jnp.int32)[:, None] == local_pos[None, :]
    cable_force = jnp.dot(
        placing.astype(jnp.bfloat16),
        sent_rows.reshape(strip_count * capacity, slab_width),
        preferred_element_type=jnp.float32,
    )
    cable_count = tension_base.shape[0]
    per_cable = strip_total // cable_count
    moved, anchor_rows = cable_update(
        displace.reshape(cable_count, per_cable, slab_width),
        displace_prev.reshape(cable_count, per_cable, slab_width),
        cable_force.reshape(cable_count, per_cable, slab_width),
        tension_base,
    )
    segment_total = seg_slot.shape[0]
    lookup = anchor_seg[:, None] == jnp.arange(segment_total, dtype=jnp.int32)[None, :]
    target_rows = jnp.sum(jnp.where(lookup, seg_slot[None, :], 0), axis=1)
    wanted = jnp.arange(segment_total // strip_count * lax.axis_size("strip"), dtype=jnp.int32)
    selector = (target_rows[None, :] == wanted[:, None]).astype(jnp.float32)
    deck_load = lax.psum_scatter(
        jnp.dot(
            selector,
            anchor_rows,
            precision=lax.Precision.HIGHEST,
            preferred_element_type=jnp.float32,
        ),
        "strip",
        scatter_dimension=0,
        tiled=True,
    )
    return (flow_out, moved.reshape(strip_total, slab_width), deck_load)


def solution(mesh):
    in_specs = (
        P("strip", None, "sub"),
        P("strip", None, "sub"),
        P("strip"),
        P("strip"),
        P("strip", "sub"),
        P("strip", "sub"),
        P("strip"),
        P("strip"),
        P(),
    )
    out_specs = (P("strip", None, "sub"), P("strip", "sub"), P("strip", "sub"))
    return jax.shard_map(
        per_device, mesh=mesh, in_specs=in_specs, out_specs=out_specs, check_vma=False
    )
```

profile of v0, /device:TPU:0, one launch (start us, length us, event | category | flops | bytes accessed | tf_op | source)
XLA Modules:
  0.0 122.8 jit_solution(1505638869812399490)
XLA Ops:
  0.6 1.9 %copy.20 = bf16[8,512,128]{1,0,2:T(8,128)(2,1)S(1)} copy(bf16[8,512,128]{2,1,0:T(8,128)(2,1)} %param.9) | data formatting | bytes 2097152 | tf_op args[0]
  2.5 1.3 %collective-permute-start = (f32[8,512,1]{1,0,2:T(8,128)S(1)}, f32[8,512,1]{1,0,2:T(8,128)S(1)}, u32[]{:S(2)}, u32[]{:S(2)}) collective-permute-start(f32[8,512,1]{1,0,2:T(8,128)S(1)} %get-tuple-element.28), channel_id=1, source_target_pairs={{1,0},{2,1},{3,2},{5,4},{6,5},{7,6},{9,8},{10,9},{11,10},{13,12},{... | collective-permute-start | bytes 49160 | tf_op jit(solution)/shard_map/ppermute | solution.py:19
  3.8 3.0 %collective-permute-start.1 = (f32[8,512,1]{1,0,2:T(8,128)S(1)}, f32[8,512,1]{1,0,2:T(8,128)S(1)}, u32[]{:S(2)}, u32[]{:S(2)}) collective-permute-start(f32[8,512,1]{1,0,2:T(8,128)S(1)} %get-tuple-element.29), channel_id=1, source_target_pairs={{0,1},{1,2},{2,3},{4,5},{5,6},{6,7},{8,9},{9,10},{10,11},{12,13},{... | collective-permute-start | bytes 49160 | tf_op jit(solution)/shard_map/ppermute | solution.py:16
  7.4 1.9 %copy.21 = bf16[8,512,128]{1,0,2:T(8,128)(2,1)S(1)} copy(bf16[8,512,128]{2,1,0:T(8,128)(2,1)} %param.10) | data formatting | bytes 2097152 | tf_op args[1]
  10.5 1.3 %collective-permute-start.2 = (f32[8,512,1]{1,0,2:T(8,128)S(1)}, f32[8,512,1]{1,0,2:T(8,128)S(1)}, u32[]{:S(2)}, u32[]{:S(2)}) collective-permute-start(f32[8,512,1]{1,0,2:T(8,128)S(1)} %get-tuple-element.26), channel_id=1, source_target_pairs={{1,0},{2,1},{3,2},{5,4},{6,5},{7,6},{9,8},{10,9},{11,10},{13,12},{... | collective-permute-start | bytes 49160 | tf_op jit(solution)/shard_map/ppermute | solution.py:19
  11.8 5.1 %collective-permute-start.3 = (f32[8,512,1]{1,0,2:T(8,128)S(1)}, f32[8,512,1]{1,0,2:T(8,128)S(1)}, u32[]{:S(2)}, u32[]{:S(2)}) collective-permute-start(f32[8,512,1]{1,0,2:T(8,128)S(1)} %get-tuple-element.27), channel_id=1, source_target_pairs={{0,1},{1,2},{2,3},{4,5},{5,6},{6,7},{8,9},{9,10},{10,11},{12,13},{... | collective-permute-start | bytes 49160 | tf_op jit(solution)/shard_map/ppermute | solution.py:16
  18.8 1.3 %collective-permute-start.4 = (f32[8,512,1]{1,0,2:T(8,128)S(1)}, f32[8,512,1]{1,0,2:T(8,128)S(1)}, u32[]{:S(2)}, u32[]{:S(2)}) collective-permute-start(f32[8,512,1]{1,0,2:T(8,128)S(1)} %get-tuple-element.24), channel_id=1, source_target_pairs={{1,0},{2,1},{3,2},{5,4},{6,5},{7,6},{9,8},{10,9},{11,10},{13,12},{... | collective-permute-start | bytes 49160 | tf_op jit(solution)/shard_map/ppermute | solution.py:19
  20.1 4.3 %collective-permute-start.5 = (f32[8,512,1]{1,0,2:T(8,128)S(1)}, f32[8,512,1]{1,0,2:T(8,128)S(1)}, u32[]{:S(2)}, u32[]{:S(2)}) collective-permute-start(f32[8,512,1]{1,0,2:T(8,128)S(1)} %get-tuple-element.25), channel_id=1, source_target_pairs={{0,1},{1,2},{2,3},{4,5},{5,6},{6,7},{8,9},{9,10},{10,11},{12,13},{... | collective-permute-start | bytes 49160 | tf_op jit(solution)/shard_map/ppermute | solution.py:16
  26.4 1.3 %collective-permute-start.6 = (f32[8,512,1]{1,0,2:T(8,128)S(1)}, f32[8,512,1]{1,0,2:T(8,128)S(1)}, u32[]{:S(2)}, u32[]{:S(2)}) collective-permute-start(f32[8,512,1]{1,0,2:T(8,128)S(1)} %get-tuple-element.22), channel_id=1, source_target_pairs={{1,0},{2,1},{3,2},{5,4},{6,5},{7,6},{9,8},{10,9},{11,10},{13,12},{... | collective-permute-start | bytes 49160 | tf_op jit(solution)/shard_map/ppermute | solution.py:19
  27.7 4.9 %collective-permute-start.7 = (f32[8,512,1]{1,0,2:T(8,128)S(1)}, f32[8,512,1]{1,0,2:T(8,128)S(1)}, u32[]{:S(2)}, u32[]{:S(2)}) collective-permute-start(f32[8,512,1]{1,0,2:T(8,128)S(1)} %get-tuple-element.23), channel_id=1, source_target_pairs={{0,1},{1,2},{2,3},{4,5},{5,6},{6,7},{8,9},{9,10},{10,11},{12,13},{... | collective-permute-start | bytes 49160 | tf_op jit(solution)/shard_map/ppermute | solution.py:16
  34.6 1.3 %collective-permute-start.8 = (f32[8,512,1]{1,0,2:T(8,128)S(1)}, f32[8,512,1]{1,0,2:T(8,128)S(1)}, u32[]{:S(2)}, u32[]{:S(2)}) collective-permute-start(f32[8,512,1]{1,0,2:T(8,128)S(1)} %get-tuple-element.20), channel_id=1, source_target_pairs={{1,0},{2,1},{3,2},{5,4},{6,5},{7,6},{9,8},{10,9},{11,10},{13,12},{... | collective-permute-start | bytes 49160 | tf_op jit(solution)/shard_map/ppermute | solution.py:19
  35.9 4.9 %collective-permute-start.9 = (f32[8,512,1]{1,0,2:T(8,128)S(1)}, f32[8,512,1]{1,0,2:T(8,128)S(1)}, u32[]{:S(2)}, u32[]{:S(2)}) collective-permute-start(f32[8,512,1]{1,0,2:T(8,128)S(1)} %get-tuple-element.21), channel_id=1, source_target_pairs={{0,1},{1,2},{2,3},{4,5},{5,6},{6,7},{8,9},{9,10},{10,11},{12,13},{... | collective-permute-start | bytes 49160 | tf_op jit(solution)/shard_map/ppermute | solution.py:16
  41.5 5.8 %all-to-all-start = ((s32[8,1,2]{2,1,0:T(1,128)}), s32[8,1,2]{2,1,0:T(1,128)S(1)}, u32[]{:S(2)}, u32[]{:S(2)}) async-start(s32[8,1,2]{2,1,0:T(1,128)} %bitcast.4), calls=%async_computation | async-start | bytes 8192 | tf_op jit(solution)/shard_map/all_to_all | solution.py:91
  49.2 1.3 %collective-permute-start.10 = (f32[8,512,1]{1,0,2:T(8,128)S(1)}, f32[8,512,1]{1,0,2:T(8,128)S(1)}, u32[]{:S(2)}, u32[]{:S(2)}) collective-permute-start(f32[8,512,1]{1,0,2:T(8,128)S(1)} %get-tuple-element.18), channel_id=1, source_target_pairs={{1,0},{2,1},{3,2},{5,4},{6,5},{7,6},{9,8},{10,9},{11,10},{13,12},{... | collective-permute-start | bytes 49160 | tf_op jit(solution)/shard_map/ppermute | solution.py:19
  50.5 4.6 %collective-permute-start.11 = (f32[8,512,1]{1,0,2:T(8,128)S(1)}, f32[8,512,1]{1,0,2:T(8,128)S(1)}, u32[]{:S(2)}, u32[]{:S(2)}) collective-permute-start(f32[8,512,1]{1,0,2:T(8,128)S(1)} %get-tuple-element.19), channel_id=1, source_target_pairs={{0,1},{1,2},{2,3},{4,5},{5,6},{6,7},{8,9},{9,10},{10,11},{12,13},{... | collective-permute-start | bytes 49160 | tf_op jit(solution)/shard_map/ppermute | solution.py:16
  57.0 1.3 %collective-permute-start.12 = (f32[8,512,1]{1,0,2:T(8,128)S(1)}, f32[8,512,1]{1,0,2:T(8,128)S(1)}, u32[]{:S(2)}, u32[]{:S(2)}) collective-permute-start(f32[8,512,1]{1,0,2:T(8,128)S(1)} %get-tuple-element.16), channel_id=1, source_target_pairs={{1,0},{2,1},{3,2},{5,4},{6,5},{7,6},{9,8},{10,9},{11,10},{13,12},{... | collective-permute-start | bytes 49160 | tf_op jit(solution)/shard_map/ppermute | solution.py:19
  58.3 4.3 %collective-permute-start.13 = (f32[8,512,1]{1,0,2:T(8,128)S(1)}, f32[8,512,1]{1,0,2:T(8,128)S(1)}, u32[]{:S(2)}, u32[]{:S(2)}) collective-permute-start(f32[8,512,1]{1,0,2:T(8,128)S(1)} %get-tuple-element.17), channel_id=1, source_target_pairs={{0,1},{1,2},{2,3},{4,5},{5,6},{6,7},{8,9},{9,10},{10,11},{12,13},{... | collective-permute-start | bytes 49160 | tf_op jit(solution)/shard_map/ppermute | solution.py:16
  64.6 1.3 %collective-permute-start.14 = (f32[8,512,1]{1,0,2:T(8,128)S(1)}, f32[8,512,1]{1,0,2:T(8,128)S(1)}, u32[]{:S(2)}, u32[]{:S(2)}) collective-permute-start(f32[8,512,1]{1,0,2:T(8,128)S(1)} %get-tuple-element.14), channel_id=1, source_target_pairs={{1,0},{2,1},{3,2},{5,4},{6,5},{7,6},{9,8},{10,9},{11,10},{13,12},{... | collective-permute-start | bytes 49160 | tf_op jit(solution)/shard_map/ppermute | solution.py:19
  65.9 5.0 %collective-permute-start.15 = (f32[8,512,1]{1,0,2:T(8,128)S(1)}, f32[8,512,1]{1,0,2:T(8,128)S(1)}, u32[]{:S(2)}, u32[]{:S(2)}) collective-permute-start(f32[8,512,1]{1,0,2:T(8,128)S(1)} %get-tuple-element.15), channel_id=1, source_target_pairs={{0,1},{1,2},{2,3},{4,5},{5,6},{6,7},{8,9},{9,10},{10,11},{12,13},{... | collective-permute-start | bytes 49160 | tf_op jit(solution)/shard_map/ppermute | solution.py:16
  72.9 2.2 %fusion.68 = (f32[8,128]{0,1:T(8,128)S(1)}, bf16[8,512,128]{1,0,2:T(8,128)(2,1)}) fusion(bf16[8,512,128]{1,0,2:T(8,128)(2,1)S(1)} %copy.21, f32[8,512,128]{1,0,2:T(8,128)S(1)} %convert_add_fusion.1, f32[8,512,1]{1,0,2:T(8,128)S(1)} %collective-permute-done.15, f32[8,512,1]{1,0,2:T(8,128)S(1)} %collective-permute-done.14, f32[8]{0:T(128)S(1)} %copy-done.1), kind=kLoop, calls=%fused_computation.132 | loop fusion | flops 6814720 | bytes 4231200 | tf_op jit(solution)/shard_map/reduce_sum | solution.py:69
  75.9 5.7 %all-to-all-start.1 = ((bf16[8,2,128]{2,1,0:T(2,128)(2,1)}), bf16[8,2,128]{2,1,0:T(2,128)(2,1)S(1)}, u32[]{:S(2)}, u32[]{:S(2)}) async-start(bf16[8,2,128]{2,1,0:T(2,128)(2,1)} %bitcast.5), calls=%async_computation.1 | async-start | bytes 8192 | tf_op jit(solution)/shard_map/all_to_all | solution.py:84
  81.7 2.7 %copy.23 = bf16[8,512,128]{2,1,0:T(8,128)(2,1)} copy(bf16[8,512,128]{1,0,2:T(8,128)(2,1)} %get-tuple-element.13) | data formatting | bytes 2097152
  84.4 3.6 %all-to-all-done.1 = bf16[8,2,128]{2,1,0:T(2,128)(2,1)S(1)} async-done(((bf16[8,2,128]{2,1,0:T(2,128)(2,1)}), bf16[8,2,128]{2,1,0:T(2,128)(2,1)S(1)}, u32[]{:S(2)}, u32[]{:S(2)}) %all-to-all-start.1) | async-done | bytes 4128 | tf_op jit(solution)/shard_map/all_to_all | solution.py:84
  88.2 33.9 %all-reduce.9 = f32[32,128]{1,0:T(8,128)S(1)} all-reduce(f32[32,128]{1,0:T(8,128)S(1)} %broadcast_multiply_fusion), channel_id=2, replica_groups=mesh['strip'=8,'sub'=4] {'strip'}, use_global_device_ids=true, to_apply=%region_6.7.clone | all-reduce | flops 4096 | bytes 32768
  (66 shorter events, 15.7 us)
Async XLA Ops:
  0.6 6.2 %copy-start.4 = (s32[8]{0:T(128)S(1)}, s32[8]{0:T(128)}, u32[]{:S(2)}) copy-start(s32[8]{0:T(128)} %param.12) | copy-start | bytes 100
  2.5 6.7 %collective-permute-start = (f32[8,512,1]{1,0,2:T(8,128)S(1)}, f32[8,512,1]{1,0,2:T(8,128)S(1)}, u32[]{:S(2)}, u32[]{:S(2)}) collective-permute-start(f32[8,512,1]{1,0,2:T(8,128)S(1)} %get-tuple-element.28), channel_id=1, source_target_pairs={{1,0},{2,1},{3,2},{5,4},{6,5},{7,6},{9,8},{10,9},{11,10},{13,12},{... | collective-permute-start | bytes 49160 | tf_op jit(solution)/shard_map/ppermute | solution.py:19
  3.8 5.4 %collective-permute-start.1 = (f32[8,512,1]{1,0,2:T(8,128)S(1)}, f32[8,512,1]{1,0,2:T(8,128)S(1)}, u32[]{:S(2)}, u32[]{:S(2)}) collective-permute-start(f32[8,512,1]{1,0,2:T(8,128)S(1)} %get-tuple-element.29), channel_id=1, source_target_pairs={{0,1},{1,2},{2,3},{4,5},{5,6},{6,7},{8,9},{9,10},{10,11},{12,13},{... | collective-permute-start | bytes 49160 | tf_op jit(solution)/shard_map/ppermute | solution.py:16
  10.5 6.4 %collective-permute-start.2 = (f32[8,512,1]{1,0,2:T(8,128)S(1)}, f32[8,512,1]{1,0,2:T(8,128)S(1)}, u32[]{:S(2)}, u32[]{:S(2)}) collective-permute-start(f32[8,512,1]{1,0,2:T(8,128)S(1)} %get-tuple-element.26), channel_id=1, source_target_pairs={{1,0},{2,1},{3,2},{5,4},{6,5},{7,6},{9,8},{10,9},{11,10},{13,12},{... | collective-permute-start | bytes 49160 | tf_op jit(solution)/shard_map/ppermute | solution.py:19
  11.8 5.9 %collective-permute-start.3 = (f32[8,512,1]{1,0,2:T(8,128)S(1)}, f32[8,512,1]{1,0,2:T(8,128)S(1)}, u32[]{:S(2)}, u32[]{:S(2)}) collective-permute-start(f32[8,512,1]{1,0,2:T(8,128)S(1)} %get-tuple-element.27), channel_id=1, source_target_pairs={{0,1},{1,2},{2,3},{4,5},{5,6},{6,7},{8,9},{9,10},{10,11},{12,13},{... | collective-permute-start | bytes 49160 | tf_op jit(solution)/shard_map/ppermute | solution.py:16
  18.8 5.7 %collective-permute-start.4 = (f32[8,512,1]{1,0,2:T(8,128)S(1)}, f32[8,512,1]{1,0,2:T(8,128)S(1)}, u32[]{:S(2)}, u32[]{:S(2)}) collective-permute-start(f32[8,512,1]{1,0,2:T(8,128)S(1)} %get-tuple-element.24), channel_id=1, source_target_pairs={{1,0},{2,1},{3,2},{5,4},{6,5},{7,6},{9,8},{10,9},{11,10},{13,12},{... | collective-permute-start | bytes 49160 | tf_op jit(solution)/shard_map/ppermute | solution.py:19
  20.1 5.1 %collective-permute-start.5 = (f32[8,512,1]{1,0,2:T(8,128)S(1)}, f32[8,512,1]{1,0,2:T(8,128)S(1)}, u32[]{:S(2)}, u32[]{:S(2)}) collective-permute-start(f32[8,512,1]{1,0,2:T(8,128)S(1)} %get-tuple-element.25), channel_id=1, source_target_pairs={{0,1},{1,2},{2,3},{4,5},{5,6},{6,7},{8,9},{9,10},{10,11},{12,13},{... | collective-permute-start | bytes 49160 | tf_op jit(solution)/shard_map/ppermute | solution.py:16
  26.4 6.3 %collective-permute-start.6 = (f32[8,512,1]{1,0,2:T(8,128)S(1)}, f32[8,512,1]{1,0,2:T(8,128)S(1)}, u32[]{:S(2)}, u32[]{:S(2)}) collective-permute-start(f32[8,512,1]{1,0,2:T(8,128)S(1)} %get-tuple-element.22), channel_id=1, source_target_pairs={{1,0},{2,1},{3,2},{5,4},{6,5},{7,6},{9,8},{10,9},{11,10},{13,12},{... | collective-permute-start | bytes 49160 | tf_op jit(solution)/shard_map/ppermute | solution.py:19
  27.7 5.7 %collective-permute-start.7 = (f32[8,512,1]{1,0,2:T(8,128)S(1)}, f32[8,512,1]{1,0,2:T(8,128)S(1)}, u32[]{:S(2)}, u32[]{:S(2)}) collective-permute-start(f32[8,512,1]{1,0,2:T(8,128)S(1)} %get-tuple-element.23), channel_id=1, source_target_pairs={{0,1},{1,2},{2,3},{4,5},{5,6},{6,7},{8,9},{9,10},{10,11},{12,13},{... | collective-permute-start | bytes 49160 | tf_op jit(solution)/shard_map/ppermute | solution.py:16
  32.7 15.2 %copy-start = (f32[8,128]{1,0:T(8,128)S(1)}, f32[8,128]{1,0:T(8,128)}, u32[]{:S(2)}) copy-start(f32[8,128]{1,0:T(8,128)} %param.13) | copy-start | bytes 12292
  34.6 13.4 %collective-permute-start.8 = (f32[8,512,1]{1,0,2:T(8,128)S(1)}, f32[8,512,1]{1,0,2:T(8,128)S(1)}, u32[]{:S(2)}, u32[]{:S(2)}) collective-permute-start(f32[8,512,1]{1,0,2:T(8,128)S(1)} %get-tuple-element.20), channel_id=1, source_target_pairs={{1,0},{2,1},{3,2},{5,4},{6,5},{7,6},{9,8},{10,9},{11,10},{13,12},{... | collective-permute-start | bytes 49160 | tf_op jit(solution)/shard_map/ppermute | solution.py:19
  35.9 12.1 %collective-permute-start.9 = (f32[8,512,1]{1,0,2:T(8,128)S(1)}, f32[8,512,1]{1,0,2:T(8,128)S(1)}, u32[]{:S(2)}, u32[]{:S(2)}) collective-permute-start(f32[8,512,1]{1,0,2:T(8,128)S(1)} %get-tuple-element.21), channel_id=1, source_target_pairs={{0,1},{1,2},{2,3},{4,5},{5,6},{6,7},{8,9},{9,10},{10,11},{12,13},{... | collective-permute-start | bytes 49160 | tf_op jit(solution)/shard_map/ppermute | solution.py:16
  41.5 34.5 %all-to-all-start = ((s32[8,1,2]{2,1,0:T(1,128)}), s32[8,1,2]{2,1,0:T(1,128)S(1)}, u32[]{:S(2)}, u32[]{:S(2)}) async-start(s32[8,1,2]{2,1,0:T(1,128)} %bitcast.4), calls=%async_computation | async-start | bytes 8192 | tf_op jit(solution)/shard_map/all_to_all | solution.py:91
  49.2 6.5 %collective-permute-start.10 = (f32[8,512,1]{1,0,2:T(8,128)S(1)}, f32[8,512,1]{1,0,2:T(8,128)S(1)}, u32[]{:S(2)}, u32[]{:S(2)}) collective-permute-start(f32[8,512,1]{1,0,2:T(8,128)S(1)} %get-tuple-element.18), channel_id=1, source_target_pairs={{1,0},{2,1},{3,2},{5,4},{6,5},{7,6},{9,8},{10,9},{11,10},{13,12},{... | collective-permute-start | bytes 49160 | tf_op jit(solution)/shard_map/ppermute | solution.py:19
  50.5 5.4 %collective-permute-start.11 = (f32[8,512,1]{1,0,2:T(8,128)S(1)}, f32[8,512,1]{1,0,2:T(8,128)S(1)}, u32[]{:S(2)}, u32[]{:S(2)}) collective-permute-start(f32[8,512,1]{1,0,2:T(8,128)S(1)} %get-tuple-element.19), channel_id=1, source_target_pairs={{0,1},{1,2},{2,3},{4,5},{5,6},{6,7},{8,9},{9,10},{10,11},{12,13},{... | collective-permute-start | bytes 49160 | tf_op jit(solution)/shard_map/ppermute | solution.py:16
  55.7 6.9 %copy-start.5 = (s32[32]{0:T(128)S(1)}, s32[32]{0:T(128)}, u32[]{:S(2)}) copy-start(s32[32]{0:T(128)} %param.17) | copy-start | bytes 388
  57.0 6.3 %collective-permute-start.12 = (f32[8,512,1]{1,0,2:T(8,128)S(1)}, f32[8,512,1]{1,0,2:T(8,128)S(1)}, u32[]{:S(2)}, u32[]{:S(2)}) collective-permute-start(f32[8,512,1]{1,0,2:T(8,128)S(1)} %get-tuple-element.16), channel_id=1, source_target_pairs={{1,0},{2,1},{3,2},{5,4},{6,5},{7,6},{9,8},{10,9},{11,10},{13,12},{... | collective-permute-start | bytes 49160 | tf_op jit(solution)/shard_map/ppermute | solution.py:19
  58.3 5.1 %collective-permute-start.13 = (f32[8,512,1]{1,0,2:T(8,128)S(1)}, f32[8,512,1]{1,0,2:T(8,128)S(1)}, u32[]{:S(2)}, u32[]{:S(2)}) collective-permute-start(f32[8,512,1]{1,0,2:T(8,128)S(1)} %get-tuple-element.17), channel_id=1, source_target_pairs={{0,1},{1,2},{2,3},{4,5},{5,6},{6,7},{8,9},{9,10},{10,11},{12,13},{... | collective-permute-start | bytes 49160 | tf_op jit(solution)/shard_map/ppermute | solution.py:16
  63.3 8.3 %copy-start.6 = (u32[32]{0:T(128)S(1)}, u32[32]{0:T(128)}, u32[]{:S(2)}) copy-start(u32[32]{0:T(128)} %constant.67) | copy-start | bytes 388
  64.6 8.2 %collective-permute-start.14 = (f32[8,512,1]{1,0,2:T(8,128)S(1)}, f32[8,512,1]{1,0,2:T(8,128)S(1)}, u32[]{:S(2)}, u32[]{:S(2)}) collective-permute-start(f32[8,512,1]{1,0,2:T(8,128)S(1)} %get-tuple-element.14), channel_id=1, source_target_pairs={{1,0},{2,1},{3,2},{5,4},{6,5},{7,6},{9,8},{10,9},{11,10},{13,12},{... | collective-permute-start | bytes 49160 | tf_op jit(solution)/shard_map/ppermute | solution.py:19
  65.9 7.0 %collective-permute-start.15 = (f32[8,512,1]{1,0,2:T(8,128)S(1)}, f32[8,512,1]{1,0,2:T(8,128)S(1)}, u32[]{:S(2)}, u32[]{:S(2)}) collective-permute-start(f32[8,512,1]{1,0,2:T(8,128)S(1)} %get-tuple-element.15), channel_id=1, source_target_pairs={{0,1},{1,2},{2,3},{4,5},{5,6},{6,7},{8,9},{9,10},{10,11},{12,13},{... | collective-permute-start | bytes 49160 | tf_op jit(solution)/shard_map/ppermute | solution.py:16
  75.1 13.0 %copy-start.3 = (f32[8,128]{1,0:T(8,128)S(1)}, f32[8,128]{1,0:T(8,128)}, u32[]{:S(2)}) copy-start(f32[8,128]{1,0:T(8,128)} %param.14) | copy-start | bytes 12292
  75.9 12.1 %all-to-all-start.1 = ((bf16[8,2,128]{2,1,0:T(2,128)(2,1)}), bf16[8,2,128]{2,1,0:T(2,128)(2,1)S(1)}, u32[]{:S(2)}, u32[]{:S(2)}) async-start(bf16[8,2,128]{2,1,0:T(2,128)(2,1)} %bitcast.5), calls=%async_computation.1 | async-start | bytes 8192 | tf_op jit(solution)/shard_map/all_to_all | solution.py:84
  88.2 34.6 %copy-start.2 = (f32[1,8,128]{2,1,0:T(8,128)}, f32[1,8,128]{2,1,0:T(8,128)S(1)}, u32[]{:S(2)}) copy-start(f32[1,8,128]{2,1,0:T(8,128)S(1)} %fusion.49) | copy-start | bytes 12292
  (1 other events, 2.2 us)
where the time goes:
time: 124 us; the launch traced here: 123 us
  starting transfers between devices  57.9 us (47%)
  blocking collectives  33.9 us (27%)
  other arithmetic  12.4 us (10%)
  local copies, waits for them, and re-layouts  8.39 us (7%)
  waiting for transfers between devices  6.2 us (5%)
  between operations  2.99 us (2%)
    ppermute x8, starting transfers between devices, padded(): lax.ppermute(lax.slice_in_dim(block, block.shape[dim] - width, None, axis...  36 us
    unnamed x1, blocking collectives  33.9 us
    ppermute x8, starting transfers between devices, padded(): lax.ppermute(lax.slice_in_dim(block, 0, width, axis=dim), axis, backward)  10.3 us
    add x7, other arithmetic, relax_edge(): return interior + rate_cells * laplace + source_cells  8.06 us
    unnamed x19, local copies, waits for them, and re-layouts  7.6 us
    all_to_all x1, starting transfers between devices, per_device(): lax.all_to_all(packed_pos.reshape(strip_count, capacity), 'strip', split_...  5.83 us
    all_to_all x1, starting transfers between devices, per_device(): lax.all_to_all(packed_rows.reshape(strip_count, capacity, slab_width), 's...  5.72 us
    all_to_all x1, waiting for transfers between devices, per_device(): lax.all_to_all(packed_rows.reshape(strip_count, capacity, slab_width), 's...  3.63 us
  transfers between devices with their start and end apart: 18, of which 6 were waited for; matrix products, arithmetic and copies ran while one was open for 12% of the time, Pallas kernels for 0%

commit v1 on v0

v1 whole, which is shorter than its diff:
```python
import functools
import math

import jax
import jax.numpy as jnp
from jax import lax
from jax.experimental import pallas as pl
from jax.experimental.pallas import tpu as pltpu
from jax.sharding import PartitionSpec as P

SWEEPS = 8
HALO = SWEEPS
LANES = 128
SUBL = 8
CHUNK = 16
MESH = pl.DeviceIdType.MESH
F32 = jnp.float32


def kernel(
    n_strip,
    n_sub,
    flow_ref,
    wall_ref,
    rate_ref,
    pos_ref,
    disp_ref,
    prev_ref,
    tens_ref,
    anchor_ref,
    slot_ref,
    out_ref,
    moved_ref,
    deck_ref,
    even,
    odd,
    source,
    staging,
    halo_out,
    halo_in,
    placed,
    placed_in,
    loads,
    loads_in,
    halo_send,
    halo_recv,
    place_send,
    place_recv,
    load_send,
    load_recv,
):
    strips, grid_rows, width = flow_ref.shape
    parts = grid_rows // LANES
    step = parts * strips
    first = HALO * step
    me = lax.axis_index("strip")
    sub = lax.axis_index("sub")
    left = lax.rem(sub + n_sub - 1, n_sub)
    right = lax.rem(sub + 1, n_sub)

    barrier = pltpu.get_barrier_semaphore()
    for neighbour in (left, right):
        pl.semaphore_signal(barrier, inc=1, device_id={"sub": neighbour}, device_id_type=MESH)
    for delta in range(1, n_strip):
        pl.semaphore_signal(
            barrier, inc=1, device_id={"strip": lax.rem(me + delta, n_strip)}, device_id_type=MESH
        )

    lane = lax.broadcasted_iota(jnp.int32, (SUBL, LANES), 1)
    subl = lax.broadcasted_iota(jnp.int32, (SUBL, LANES), 0)
    zero = jnp.zeros((SUBL, LANES), F32)

    for index, (array, target) in enumerate(((flow_ref, even), (wall_ref, source))):
        for strip in range(strips):
            stage = (index * strips + strip) % 2
            staging[stage] = array[strip].astype(F32)
            for part in range(parts):
                block = staging[stage, pl.ds(part, LANES, stride=parts), :]
                target[pl.ds(first + part * strips + strip, width, stride=step), :] = block.T

    rows = HALO * step
    last = first + (width - HALO) * step
    for side, start in ((0, first), (1, last)):
        halo_out[side, 0:rows] = even[start : start + rows].astype(jnp.bfloat16)
        halo_out[side, rows : 2 * rows] = source[start : start + rows].astype(jnp.bfloat16)
    pl.semaphore_wait(barrier, n_strip - 1 + 2)
    halos = []
    for side, neighbour in ((0, left), (1, right)):
        copy = pltpu.make_async_remote_copy(
            src_ref=halo_out.at[side],
            dst_ref=halo_in.at[1 - side],
            send_sem=halo_send.at[side],
            recv_sem=halo_recv.at[1 - side],
            device_id={"sub": neighbour},
            device_id_type=MESH,
        )
        copy.start()
        halos.append(copy)

    rate = zero
    for strip in range(strips):
        rate = jnp.where(subl == strip, rate_ref[strip], rate)
    keep = 1.0 - 4.0 * rate
    has_left = jnp.where(sub > 0, 1.0, 0.0).astype(F32)
    has_right = jnp.where(sub < n_sub - 1, 1.0, 0.0).astype(F32)
    rate_left, rate_right = rate * has_left, rate * has_right
    keep_left, keep_right = 1.0 - 4.0 * rate_left, 1.0 - 4.0 * rate_right
    at_top, at_bottom = lane == 0, lane == LANES - 1

    def relax(old, new, start, columns, factors):
        def cells(ref, column):
            return [
                ref[pl.ds(start + column * step + part * strips, strips), :]
                for part in range(parts)
            ]

        before, here = cells(old, -1), cells(old, 0)
        for u in range(columns):
            after = cells(old, u + 1)
            walls = cells(source, u)
            scale, weight = factors(u)
            for part in range(parts):
                if part > 0:
                    up = here[part - 1]
                else:
                    up = jnp.where(at_top, 0.0, pltpu.roll(here[parts - 1], 1, 1))
                if part < parts - 1:
                    down = here[part + 1]
                else:
                    down = jnp.where(at_bottom, 0.0, pltpu.roll(here[0], LANES - 1, 1))
                around = (before[part] + after[part]) + (up + down)
                new[pl.ds(start + u * step + part * strips, strips), :] = (
                    scale * here[part] + walls[part]
                ) + weight * around
            before, here = here, after

    inner = lambda u: (keep, rate)
    buffers = (even, odd)

    chunks = (width - 2 * HALO) // CHUNK
    for sweep in range(1, SWEEPS + 1):
        old, new = buffers[(sweep - 1) % 2], buffers[sweep % 2]

        def body(chunk, carry, old=old, new=new):
            start = pl.multiple_of(2 * first + chunk * (CHUNK * step), CHUNK * step)
            relax(old, new, start, CHUNK, inner)
            return carry

        lax.fori_loop(0, chunks, body, 0)
        side = HALO - sweep
        if side:
            relax(old, new, first + sweep * step, side, inner)
            relax(old, new, first + (width - HALO) * step, side, inner)

    for copy in halos:
        copy.wait()
    for side, start, mask in ((0, 0, has_left), (1, first + width * step, has_right)):
        even[start : start + rows] = halo_in[side, 0:rows].astype(F32) * mask
        source[start : start + rows] = halo_in[side, rows : 2 * rows].astype(F32) * mask
    for sweep in range(1, SWEEPS + 1):
        old, new = buffers[(sweep - 1) % 2], buffers[sweep % 2]
        relax(
            old,
            new,
            sweep * step,
            HALO,
            lambda u: (keep_left, rate_left) if u + sweep < HALO else (keep, rate),
        )
        relax(
            old,
            new,
            first + (width - sweep) * step,
            HALO,
            lambda u: (keep_right, rate_right) if u >= sweep else (keep, rate),
        )
    final = buffers[SWEEPS % 2]

    force = []
    for strip in range(strips):
        total = None
        for part in range(parts):
            block = final[pl.ds(first + part * strips + strip, width, stride=step), :]
            total = block if total is None else total + block
        row = jnp.sum(total.T, axis=0, keepdims=True) * (1.0 / math.sqrt(grid_rows))
        force.append(row.astype(jnp.bfloat16).astype(F32))
    for owner in range(n_strip):
        tile = zero
        for strip in range(strips):
            tile = tile + jnp.where(subl + owner * strips == pos_ref[strip], force[strip], 0.0)
        placed[owner] = tile

    def exchange(tiles, landing, send_sems, recv_sems):
        copies = []
        for delta in range(1, n_strip):
            target = lax.rem(me + delta, n_strip)
            copy = pltpu.make_async_remote_copy(
                src_ref=tiles.at[target],
                dst_ref=landing.at[delta],
                send_sem=send_sems.at[delta],
                recv_sem=recv_sems.at[delta],
                device_id={"strip": target},
                device_id_type=MESH,
            )
            copy.start()
            copies.append(copy)
        return copies

    copies = exchange(placed, placed_in, place_send, place_recv)

    for strip in range(strips):
        stage = strip % 2
        for part in range(parts):
            block = final[pl.ds(first + part * strips + strip, width, stride=step), :]
            staging[stage, pl.ds(part, LANES, stride=parts), :] = block.T
        out_ref[strip] = staging[stage].astype(jnp.bfloat16)

    u = disp_ref[...]
    above = jnp.where(subl == 0, 0.0, pltpu.roll(u, 1, 0))
    below = jnp.where(subl == SUBL - 1, 0.0, pltpu.roll(u, SUBL - 1, 0))
    slope = u - above
    squares = slope * slope + jnp.where(subl == SUBL - 1, u * u, 0.0)
    stretch = jnp.sum(squares, axis=0, keepdims=True) * (1.0 / (SUBL + 1))
    tension = tens_ref[0] * (1.0 + stretch)
    moved = 2.0 * u - prev_ref[...] + tension * (below - 2.0 * u + above)

    cable_force = placed[me]
    for delta, copy in enumerate(copies, 1):
        copy.wait()
        cable_force = cable_force + placed_in[delta]
    moved = moved + 0.5 * cable_force
    moved_ref[...] = moved
    anchor = tension * moved[0:1, :]

    deck_rows = deck_ref.shape[0]
    wanted = slot_ref[anchor_ref[0]]
    for owner in range(n_strip):
        hit = (subl + owner * deck_rows == wanted) & (subl < deck_rows)
        loads[owner] = jnp.where(hit, anchor, 0.0)
    copies = exchange(loads, loads_in, load_send, load_recv)
    total = loads[me]
    for delta, copy in enumerate(copies, 1):
        copy.wait()
        total = total + loads_in[delta]
    deck_ref[...] = total[0:deck_rows, :]


def per_device(n_strip, n_sub, *args):
    flow_field, _, _, _, displace = args[:5]
    seg_slot = args[8]
    strips, grid_rows, width = flow_field.shape
    step = grid_rows // LANES * strips
    rows = (width + 2 * HALO) * step
    deck_rows = seg_slot.shape[0] // n_strip
    vmem = pl.BlockSpec(memory_space=pltpu.VMEM)
    smem = pl.BlockSpec(memory_space=pltpu.SMEM)
    dma = pltpu.SemaphoreType.DMA
    return pl.pallas_call(
        functools.partial(kernel, n_strip, n_sub),
        out_shape=(
            jax.ShapeDtypeStruct(flow_field.shape, jnp.bfloat16),
            jax.ShapeDtypeStruct(displace.shape, F32),
            jax.ShapeDtypeStruct((deck_rows, width), F32),
        ),
        in_specs=[vmem, vmem, smem, smem, vmem, vmem, smem, smem, smem],
        out_specs=(vmem, vmem, vmem),
        scratch_shapes=[
            pltpu.VMEM((rows, LANES), F32),
            pltpu.VMEM((rows, LANES), F32),
            pltpu.VMEM((rows, LANES), F32),
            pltpu.VMEM((2, grid_rows, LANES), F32),
            pltpu.VMEM((2, 2 * HALO * step, LANES), jnp.bfloat16),
            pltpu.VMEM((2, 2 * HALO * step, LANES), jnp.bfloat16),
            pltpu.VMEM((n_strip, SUBL, LANES), F32),
            pltpu.VMEM((n_strip, SUBL, LANES), F32),
            pltpu.VMEM((n_strip, SUBL, LANES), F32),
            pltpu.VMEM((n_strip, SUBL, LANES), F32),
            dma((2,)),
            dma((2,)),
            dma((n_strip,)),
            dma((n_strip,)),
            dma((n_strip,)),
            dma((n_strip,)),
        ],
        compiler_params=pltpu.CompilerParams(
            collective_id=0, has_side_effects=True, vmem_limit_bytes=32 * 1024 * 1024
        ),
    )(*args)


def solution(mesh):
    in_specs = (
        P("strip", None, "sub"),
        P("strip", None, "sub"),
        P("strip"),
        P("strip"),
        P("strip", "sub"),
        P("strip", "sub"),
        P("strip"),
        P("strip"),
        P(),
    )
    out_specs = (P("strip", None, "sub"), P("strip", "sub"), P("strip", "sub"))
    return jax.shard_map(
        functools.partial(per_device, mesh.shape["strip"], mesh.shape["sub"]),
        mesh=mesh,
        in_specs=in_specs,
        out_specs=out_specs,
        check_vma=False,
    )
```

time: 124 us -> 31.7 us (0.26)
  starting transfers between devices: 57.9 us -> 0 us
  blocking collectives: 33.9 us -> 0 us
  Pallas kernels: 0 us -> 23.4 us
  other arithmetic: 12.4 us -> 0 us
  waiting for transfers between devices: 6.2 us -> 0 us
  local copies, waits for them, and re-layouts: 8.39 us -> 5.97 us
    ppermute x16 -> x0, starting transfers between devices: 46.4 us -> none  [the longest x8 36 us: padded(): lax.ppermute(lax.slice_in_dim(block, block.shape[dim] - width, None, axis...]
    unnamed x1 -> x0, blocking collectives: 33.9 us -> none
    pallas_call x0 -> x1, Pallas kernels: none -> 23.4 us  [per_device(): pl.pallas_call(functools.partial(kernel, n_strip, n_sub), out_shape=(jax....]
    all_to_all x2 -> x0, starting transfers between devices: 11.6 us -> none  [the longest x1 5.83 us: per_device(): lax.all_to_all(packed_pos.reshape(strip_count, capacity), 'strip', split_...]
    add x8 -> x0, other arithmetic: 8.07 us -> none  [the longest x7 8.06 us: relax_edge(): return interior + rate_cells * laplace + source_cells]
    all_to_all x2 -> x0, waiting for transfers between devices: 3.64 us -> none  [the longest x1 3.63 us: per_device(): lax.all_to_all(packed_rows.reshape(strip_count, capacity, slab_width), 's...]
    reduce_sum x5 -> x0, other arithmetic: 3.16 us -> none  [the longest x1 2.22 us: per_device(): jnp.sum(values, axis=1) * (1.0 / math.sqrt(grid_rows))]
    ppermute x16 -> x0, waiting for transfers between devices: 2.57 us -> none  [the longest x8 2.54 us: padded(): lax.ppermute(lax.slice_in_dim(block, block.shape[dim] - width, None, axis...]
  transfers between devices with their start and end apart: 18 -> 0, of which waited for: 6 -> 0; matrix products, arithmetic and copies ran while one was open for 12% -> 0% of each run, Pallas kernels for 0% -> 0%
where the time goes in v1:
time: 31.7 us; the launch traced here: 31.4 us
  Pallas kernels  23.4 us (74%)
  local copies, waits for them, and re-layouts  5.97 us (19%)
  between operations  2.02 us (6%)
    pallas_call x1, Pallas kernels, per_device(): pl.pallas_call(functools.partial(kernel, n_strip, n_sub), out_shape=(jax....  23.4 us
    unnamed x17, local copies, waits for them, and re-layouts  5.97 us

profile of v1, /device:TPU:0, one launch (start us, length us, event | category | flops | bytes accessed | tf_op | source)
XLA Modules:
  0.0 31.4 jit_solution(17039838978430841982)
XLA Ops:
  1.3 0.0 copy-start.4
  1.3 0.0 copy-start.5
  1.3 0.0 copy-start.6
  2.0 0.0 copy-done.4
  2.0 0.0 copy-done.5
  2.0 0.0 copy-done.6
  2.0 0.0 copy-start
  2.0 1.2 %copy-done = bf16[8,512,128]{2,1,0:T(8,128)(2,1)S(1)} copy-done((bf16[8,512,128]{2,1,0:T(8,128)(2,1)S(1)}, bf16[8,512,128]{2,1,0:T(8,128)(2,1)}, u32[]{:S(2)}) %copy-start) | copy-done | bytes 1048600
  3.2 0.0 copy-start.1
  3.2 1.2 %copy-done.1 = bf16[8,512,128]{2,1,0:T(8,128)(2,1)S(1)} copy-done((bf16[8,512,128]{2,1,0:T(8,128)(2,1)S(1)}, bf16[8,512,128]{2,1,0:T(8,128)(2,1)}, u32[]{:S(2)}) %copy-start.1) | copy-done | bytes 1048600
  4.5 0.0 copy-start.2
  4.5 0.7 %copy-done.2 = f32[8,128]{1,0:T(8,128)S(1)} copy-done((f32[8,128]{1,0:T(8,128)S(1)}, f32[8,128]{1,0:T(8,128)}, u32[]{:S(2)}) %copy-start.2) | copy-done | bytes 4120
  5.1 0.0 copy-start.3
  5.2 0.7 %copy-done.3 = f32[8,128]{1,0:T(8,128)S(1)} copy-done((f32[8,128]{1,0:T(8,128)S(1)}, f32[8,128]{1,0:T(8,128)}, u32[]{:S(2)}) %copy-start.3) | copy-done | bytes 4120
  5.8 23.4 %shard_map.112 = (bf16[8,512,128]{2,1,0:T(8,128)(2,1)S(1)}, f32[8,128]{1,0:T(8,128)S(1)}, f32[4,128]{1,0:T(4,128)S(1)}) custom-call(bf16[8,512,128]{2,1,0:T(8,128)(2,1)S(1)} %copy-done, bf16[8,512,128]{2,1,0:T(8,128)(2,1)S(1)} %copy-done.1, f32[8]{0:T(128)S(1)} %copy-done.4, s32[8]{0:T(128)S(1)} %copy-done.5, f32[8,128]{1,0:T(8,128)S(1)} %copy-done.2, ...), custom_call_target="tpu_custom_call" | custom-call | tf_op jit(solution)/shard_map/pallas_call | solution.py:257
  29.2 1.0 %copy.17 = bf16[8,512,128]{2,1,0:T(8,128)(2,1)} copy(bf16[8,512,128]{2,1,0:T(8,128)(2,1)S(1)} %get-tuple-element.6) | data formatting | bytes 2097152
  30.2 0.6 %copy.18 = f32[8,128]{1,0:T(8,128)} copy(f32[8,128]{1,0:T(8,128)S(1)} %get-tuple-element.7) | data formatting | bytes 8192
  30.8 0.6 %copy.19 = f32[4,128]{1,0:T(4,128)} copy(f32[4,128]{1,0:T(4,128)S(1)} %get-tuple-element.8) | data formatting | bytes 4096
Async XLA Ops:
  1.3 0.7 %copy-start.4 = (f32[8]{0:T(128)S(1)}, f32[8]{0:T(128)}, u32[]{:S(2)}) copy-start(f32[8]{0:T(128)} %rate_ref.1) | copy-start | bytes 100
  1.3 0.7 %copy-start.5 = (s32[8]{0:T(128)S(1)}, s32[8]{0:T(128)}, u32[]{:S(2)}) copy-start(s32[8]{0:T(128)} %pos_ref.1) | copy-start | bytes 100
  1.3 0.7 %copy-start.6 = (s32[32]{0:T(128)S(1)}, s32[32]{0:T(128)}, u32[]{:S(2)}) copy-start(s32[32]{0:T(128)} %slot_ref.1) | copy-start | bytes 388
  2.0 1.2 %copy-start = (bf16[8,512,128]{2,1,0:T(8,128)(2,1)S(1)}, bf16[8,512,128]{2,1,0:T(8,128)(2,1)}, u32[]{:S(2)}) copy-start(bf16[8,512,128]{2,1,0:T(8,128)(2,1)} %flow_ref.1) | copy-start | bytes 3145732
  3.2 1.2 %copy-start.1 = (bf16[8,512,128]{2,1,0:T(8,128)(2,1)S(1)}, bf16[8,512,128]{2,1,0:T(8,128)(2,1)}, u32[]{:S(2)}) copy-start(bf16[8,512,128]{2,1,0:T(8,128)(2,1)} %wall_ref.1) | copy-start | bytes 3145732
  4.5 0.7 %copy-start.2 = (f32[8,128]{1,0:T(8,128)S(1)}, f32[8,128]{1,0:T(8,128)}, u32[]{:S(2)}) copy-start(f32[8,128]{1,0:T(8,128)} %disp_ref.1) | copy-start | bytes 12292
  5.1 0.7 %copy-start.3 = (f32[8,128]{1,0:T(8,128)S(1)}, f32[8,128]{1,0:T(8,128)}, u32[]{:S(2)}) copy-start(f32[8,128]{1,0:T(8,128)} %prev_ref.1) | copy-start | bytes 12292

commit v2 on v1

--- a/solution.py
+++ b/solution.py
@@ -12,7 +12,7 @@
 HALO = SWEEPS
 LANES = 128
 SUBL = 8
-CHUNK = 16
+CHUNK = 28
 MESH = pl.DeviceIdType.MESH
 F32 = jnp.float32
 
@@ -20,16 +20,16 @@
 def kernel(
     n_strip,
     n_sub,
-    flow_ref,
-    wall_ref,
+    flow_hbm,
+    wall_hbm,
     rate_ref,
     pos_ref,
-    disp_ref,
-    prev_ref,
+    disp_hbm,
+    prev_hbm,
     tens_ref,
     anchor_ref,
     slot_ref,
-    out_ref,
+    out_hbm,
     moved_ref,
     deck_ref,
     even,
@@ -38,18 +38,39 @@
     staging,
     halo_out,
     halo_in,
-    placed,
-    placed_in,
-    loads,
-    loads_in,
+    tiles,
+    tiles_in,
+    info,
+    info_in,
+    flow_ref,
+    wall_ref,
+    disp_ref,
+    prev_ref,
+    out_ref,
     halo_send,
     halo_recv,
-    place_send,
-    place_recv,
-    load_send,
-    load_recv,
+    tile_send,
+    tile_recv,
+    info_send,
+    info_recv,
+    in_sem,
+    small_sem,
+    out_sem,
 ):
     strips, grid_rows, width = flow_ref.shape
+    arriving = [
+        [
+            pltpu.make_async_copy(array.at[strip], target.at[strip], in_sem.at[index, strip])
+            for strip in range(strips)
+        ]
+        for index, (array, target) in enumerate(((flow_hbm, flow_ref), (wall_hbm, wall_ref)))
+    ]
+    small = [
+        pltpu.make_async_copy(array, target, small_sem.at[index])
+        for index, (array, target) in enumerate(((disp_hbm, disp_ref), (prev_hbm, prev_ref)))
+    ]
+    for copy in small + arriving[0] + arriving[1]:
+        copy.start()
     parts = grid_rows // LANES
     step = parts * strips
     first = HALO * step
@@ -73,6 +94,7 @@
     for index, (array, target) in enumerate(((flow_ref, even), (wall_ref, source))):
         for strip in range(strips):
             stage = (index * strips + strip) % 2
+            arriving[index][strip].wait()
             staging[stage] = array[strip].astype(F32)
             for part in range(parts):
                 block = staging[stage, pl.ds(part, LANES, stride=parts), :]
@@ -96,6 +118,40 @@
         )
         copy.start()
         halos.append(copy)
+
+    for copy in small:
+        copy.wait()
+    u = disp_ref[...]
+    above = jnp.where(subl == 0, 0.0, pltpu.roll(u, 1, 0))
+    below = jnp.where(subl == SUBL - 1, 0.0, pltpu.roll(u, SUBL - 1, 0))
+    slope = u - above
+    squares = slope * slope + jnp.where(subl == SUBL - 1, u * u, 0.0)
+    stretch = jnp.sum(squares, axis=0, keepdims=True) * (1.0 / (SUBL + 1))
+    tension = tens_ref[0] * (1.0 + stretch)
+    moved = 2.0 * u - prev_ref[...] + tension * (below - 2.0 * u + above)
+
+    wanted = slot_ref[anchor_ref[0]].astype(F32)
+    info[0:1, :] = tension
+    info[1:2, :] = tension * moved[0:1, :]
+    info[2:SUBL, :] = jnp.full((SUBL - 2, LANES), wanted, F32)
+
+    def exchange(source_of, landing, send_sems, recv_sems):
+        copies = []
+        for delta in range(1, n_strip):
+            target = lax.rem(me + delta, n_strip)
+            copy = pltpu.make_async_remote_copy(
+                src_ref=source_of(target),
+                dst_ref=landing.at[delta],
+                send_sem=send_sems.at[delta],
+                recv_sem=recv_sems.at[delta],
+                device_id={"strip": target},
+                device_id_type=MESH,
+            )
+            copy.start()
+            copies.append(copy)
+        return copies
+
+    sent = exchange(lambda target: info, info_in, info_send, info_recv)
 
     rate = zero
     for strip in range(strips):
@@ -142,7 +198,7 @@
         old, new = buffers[(sweep - 1) % 2], buffers[sweep % 2]
 
         def body(chunk, carry, old=old, new=new):
-            start = pl.multiple_of(2 * first + chunk * (CHUNK * step), CHUNK * step)
+            start = pl.multiple_of(2 * first + chunk * (CHUNK * step), 4 * step)
             relax(old, new, start, CHUNK, inner)
             return carry
 
@@ -187,61 +243,52 @@
         tile = zero
         for strip in range(strips):
             tile = tile + jnp.where(subl + owner * strips == pos_ref[strip], force[strip], 0.0)
-        placed[owner] = tile
-
-    def exchange(tiles, landing, send_sems, recv_sems):
-        copies = []
-        for delta in range(1, n_strip):
-            target = lax.rem(me + delta, n_strip)
-            copy = pltpu.make_async_remote_copy(
-                src_ref=tiles.at[target],
-                dst_ref=landing.at[delta],
-                send_sem=send_sems.at[delta],
-                recv_sem=recv_sems.at[delta],
-                device_id={"strip": target},
-                device_id_type=MESH,
-            )
-            copy.start()
-            copies.append(copy)
-        return copies
-
-    copies = exchange(placed, placed_in, place_send, place_recv)
-
+        tiles[owner, 0:SUBL] = tile
+
+    for copy in sent:
+        copy.wait()
+    deck_rows = deck_ref.shape[0]
+    subf = jnp.where(subl < deck_rows, subl, -(2**20)).astype(F32)
+    cables = []
+    for delta in range(n_strip):
+        told = info if delta == 0 else info_in.at[delta]
+        at_first = tiles[lax.rem(me + n_strip - delta, n_strip), 0:1]
+        row, base = told[2:3, :], told[1:2, :]
+        cables.append((row, base, 0.5 * told[0:1, :] * at_first))
+    for owner in range(n_strip):
+        tile = zero
+        for row, base, share in cables:
+            tile = tile + jnp.where(subf + float(owner * deck_rows) == row, share, 0.0)
+        tiles[owner, SUBL : 2 * SUBL] = tile
+
+    copies = exchange(lambda target: tiles.at[target], tiles_in, tile_send, tile_recv)
+
+    mine = (me * deck_rows).astype(F32)
+    total = zero
+    for row, base, share in cables:
+        total = total + jnp.where(subf + mine == row, base, 0.0)
+
+    leaving = []
     for strip in range(strips):
         stage = strip % 2
         for part in range(parts):
             block = final[pl.ds(first + part * strips + strip, width, stride=step), :]
             staging[stage, pl.ds(part, LANES, stride=parts), :] = block.T
         out_ref[strip] = staging[stage].astype(jnp.bfloat16)
-
-    u = disp_ref[...]
-    above = jnp.where(subl == 0, 0.0, pltpu.roll(u, 1, 0))
-    below = jnp.where(subl == SUBL - 1, 0.0, pltpu.roll(u, SUBL - 1, 0))
-    slope = u - above
-    squares = slope * slope + jnp.where(subl == SUBL - 1, u * u, 0.0)
-    stretch = jnp.sum(squares, axis=0, keepdims=True) * (1.0 / (SUBL + 1))
-    tension = tens_ref[0] * (1.0 + stretch)
-    moved = 2.0 * u - prev_ref[...] + tension * (below - 2.0 * u + above)
-
-    cable_force = placed[me]
+        copy = pltpu.make_async_copy(out_ref.at[strip], out_hbm.at[strip], out_sem.at[strip])
+        copy.start()
+        leaving.append(copy)
+
+    cable_force = tiles[me, 0:SUBL]
+    total = total + tiles[me, SUBL : 2 * SUBL]
     for delta, copy in enumerate(copies, 1):
         copy.wait()
-        cable_force = cable_force + placed_in[delta]
-    moved = moved + 0.5 * cable_force
-    moved_ref[...] = moved
-    anchor = tension * moved[0:1, :]
-
-    deck_rows = deck_ref.shape[0]
-    wanted = slot_ref[anchor_ref[0]]
-    for owner in range(n_strip):
-        hit = (subl + owner * deck_rows == wanted) & (subl < deck_rows)
-        loads[owner] = jnp.where(hit, anchor, 0.0)
-    copies = exchange(loads, loads_in, load_send, load_recv)
-    total = loads[me]
-    for delta, copy in enumerate(copies, 1):
-        copy.wait()
-        total = total + loads_in[delta]
+        cable_force = cable_force + tiles_in[delta, 0:SUBL]
+        total = total + tiles_in[delta, SUBL : 2 * SUBL]
+    moved_ref[...] = moved + 0.5 * cable_force
     deck_ref[...] = total[0:deck_rows, :]
+    for copy in leaving:
+        copy.wait()
 
 
 def per_device(n_strip, n_sub, *args):
@@ -252,6 +299,7 @@
     rows = (width + 2 * HALO) * step
     deck_rows = seg_slot.shape[0] // n_strip
     vmem = pl.BlockSpec(memory_space=pltpu.VMEM)
+    anywhere = pl.BlockSpec(memory_space=pl.ANY)
     smem = pl.BlockSpec(memory_space=pltpu.SMEM)
     dma = pltpu.SemaphoreType.DMA
     return pl.pallas_call(
@@ -261,8 +309,8 @@
             jax.ShapeDtypeStruct(displace.shape, F32),
             jax.ShapeDtypeStruct((deck_rows, width), F32),
         ),
-        in_specs=[vmem, vmem, smem, smem, vmem, vmem, smem, smem, smem],
-        out_specs=(vmem, vmem, vmem),
+        in_specs=[anywhere, anywhere, smem, smem, anywhere, anywhere, smem, smem, smem],
+        out_specs=(anywhere, vmem, vmem),
         scratch_shapes=[
             pltpu.VMEM((rows, LANES), F32),
             pltpu.VMEM((rows, LANES), F32),
@@ -270,19 +318,27 @@
             pltpu.VMEM((2, grid_rows, LANES), F32),
             pltpu.VMEM((2, 2 * HALO * step, LANES), jnp.bfloat16),
             pltpu.VMEM((2, 2 * HALO * step, LANES), jnp.bfloat16),
+            pltpu.VMEM((n_strip, 2 * SUBL, LANES), F32),
+            pltpu.VMEM((n_strip, 2 * SUBL, LANES), F32),
+            pltpu.VMEM((SUBL, LANES), F32),
             pltpu.VMEM((n_strip, SUBL, LANES), F32),
-            pltpu.VMEM((n_strip, SUBL, LANES), F32),
-            pltpu.VMEM((n_strip, SUBL, LANES), F32),
-            pltpu.VMEM((n_strip, SUBL, LANES), F32),
+            pltpu.VMEM(flow_field.shape, jnp.bfloat16),
+            pltpu.VMEM(flow_field.shape, jnp.bfloat16),
+            pltpu.VMEM(displace.shape, F32),
+            pltpu.VMEM(displace.shape, F32),
+            pltpu.VMEM(flow_field.shape, jnp.bfloat16),
             dma((2,)),
             dma((2,)),
             dma((n_strip,)),
             dma((n_strip,)),
             dma((n_strip,)),
             dma((n_strip,)),
+            dma((2, strips)),
+            dma((2,)),
+            dma((strips,)),
         ],
         compiler_params=pltpu.CompilerParams(
-            collective_id=0, has_side_effects=True, vmem_limit_bytes=32 * 1024 * 1024
+            collective_id=0, has_side_effects=True, vmem_limit_bytes=56 * 1024 * 1024
         ),
     )(*args)
 

time: 31.7 us -> 27 us (0.85)
  local copies, waits for them, and re-layouts: 5.97 us -> 3.53 us
  Pallas kernels: 23.4 us -> 21.3 us
    unnamed x17 -> x7, local copies, waits for them, and re-layouts: 5.97 us -> 3.53 us
    pallas_call x1, Pallas kernels: 23.4 us -> 21.3 us  [per_device(): pl.pallas_call(functools.partial(kernel, n_strip, n_sub), out_shape=(jax....]
where the time goes in v2:
time: 27 us; the launch traced here: 26.8 us
  Pallas kernels  21.3 us (79%)
  local copies, waits for them, and re-layouts  3.53 us (13%)
  between operations  1.94 us (7%)
    pallas_call x1, Pallas kernels, per_device(): pl.pallas_call(functools.partial(kernel, n_strip, n_sub), out_shape=(jax....  21.3 us
    unnamed x7, local copies, waits for them, and re-layouts  3.53 us

profile of v2, /device:TPU:0, one launch (start us, length us, event | category | flops | bytes accessed | tf_op | source)
XLA Modules:
  0.0 26.8 jit_solution(17759256841199952798)
XLA Ops:
  1.9 21.3 %shard_map.112 = (bf16[8,512,128]{2,1,0:T(8,128)(2,1)}, f32[8,128]{1,0:T(8,128)}, f32[4,128]{1,0:T(4,128)}) custom-call(bf16[8,512,128]{2,1,0:T(8,128)(2,1)} %flow_hbm.1, bf16[8,512,128]{2,1,0:T(8,128)(2,1)} %wall_hbm.1, f32[8]{0:T(128)} %rate_ref.1, s32[8]{0:T(128)} %pos_ref.1, f32[8,128]{1,0:T(8,128)} %disp_hbm.1, f32[8,128]{1,0:T(8,128)} %prev_hbm.1, ...), custom_call_target="tpu_custom_call" | custom-call | tf_op jit(solution)/shard_map/pallas_call | solution.py:305
  23.2 0.0 copy-start
  23.2 2.3 %copy.17 = bf16[8,512,128]{2,1,0:T(8,128)(2,1)} copy(bf16[8,512,128]{2,1,0:T(8,128)(2,1)} %get-tuple-element.6) | data formatting | bytes 2097152
  25.5 0.0 copy-done
  25.5 0.0 copy-start.1
  25.5 0.6 %copy.18 = f32[8,128]{1,0:T(8,128)} copy(f32[8,128]{1,0:T(8,128)S(1)} %copy-done) | data formatting | bytes 8192
  26.1 0.1 copy-done.1
  26.2 0.6 %copy.19 = f32[4,128]{1,0:T(4,128)} copy(f32[4,128]{1,0:T(4,128)S(1)} %copy-done.1) | data formatting | bytes 4096
Async XLA Ops:
  23.2 2.3 %copy-start = (f32[8,128]{1,0:T(8,128)S(1)}, f32[8,128]{1,0:T(8,128)}, u32[]{:S(2)}) copy-start(f32[8,128]{1,0:T(8,128)} %get-tuple-element.7) | copy-start | bytes 12292
  25.5 0.7 %copy-start.1 = (f32[4,128]{1,0:T(4,128)S(1)}, f32[4,128]{1,0:T(4,128)}, u32[]{:S(2)}) copy-start(f32[4,128]{1,0:T(4,128)} %get-tuple-element.8) | copy-start | bytes 6148

commit v3 on v2

--- a/solution.py
+++ b/solution.py
@@ -12,7 +12,7 @@
 HALO = SWEEPS
 LANES = 128
 SUBL = 8
-CHUNK = 28
+CHUNK = 56
 MESH = pl.DeviceIdType.MESH
 F32 = jnp.float32
 

time: 27 us -> 26.6 us (0.985)
  Pallas kernels: 21.3 us -> 20.9 us
    pallas_call x1, Pallas kernels: 21.3 us -> 20.9 us  [per_device(): pl.pallas_call(functools.partial(kernel, n_strip, n_sub), out_shape=(jax....]
where the time goes in v3:
time: 26.6 us; the launch traced here: 26.4 us
  Pallas kernels  20.9 us (79%)
  local copies, waits for them, and re-layouts  3.53 us (13%)
  between operations  1.94 us (7%)
    pallas_call x1, Pallas kernels, per_device(): pl.pallas_call(functools.partial(kernel, n_strip, n_sub), out_shape=(jax....  20.9 us
    unnamed x7, local copies, waits for them, and re-layouts  3.53 us

profile of v3, /device:TPU:0, one launch (start us, length us, event | category | flops | bytes accessed | tf_op | source)
XLA Modules:
  0.0 26.4 jit_solution(16671299701548973074)
XLA Ops:
  1.9 20.9 %shard_map.112 = (bf16[8,512,128]{2,1,0:T(8,128)(2,1)}, f32[8,128]{1,0:T(8,128)}, f32[4,128]{1,0:T(4,128)}) custom-call(bf16[8,512,128]{2,1,0:T(8,128)(2,1)} %flow_hbm.1, bf16[8,512,128]{2,1,0:T(8,128)(2,1)} %wall_hbm.1, f32[8]{0:T(128)} %rate_ref.1, s32[8]{0:T(128)} %pos_ref.1, f32[8,128]{1,0:T(8,128)} %disp_hbm.1, f32[8,128]{1,0:T(8,128)} %prev_hbm.1, ...), custom_call_target="tpu_custom_call" | custom-call | tf_op jit(solution)/shard_map/pallas_call | solution.py:305
  22.8 0.0 copy-start
  22.9 2.3 %copy.17 = bf16[8,512,128]{2,1,0:T(8,128)(2,1)} copy(bf16[8,512,128]{2,1,0:T(8,128)(2,1)} %get-tuple-element.6) | data formatting | bytes 2097152
  25.1 0.0 copy-done
  25.1 0.0 copy-start.1
  25.1 0.6 %copy.18 = f32[8,128]{1,0:T(8,128)} copy(f32[8,128]{1,0:T(8,128)S(1)} %copy-done) | data formatting | bytes 8192
  25.7 0.1 copy-done.1
  25.8 0.6 %copy.19 = f32[4,128]{1,0:T(4,128)} copy(f32[4,128]{1,0:T(4,128)S(1)} %copy-done.1) | data formatting | bytes 4096
Async XLA Ops:
  22.8 2.3 %copy-start = (f32[8,128]{1,0:T(8,128)S(1)}, f32[8,128]{1,0:T(8,128)}, u32[]{:S(2)}) copy-start(f32[8,128]{1,0:T(8,128)} %get-tuple-element.7) | copy-start | bytes 12292
  25.1 0.7 %copy-start.1 = (f32[4,128]{1,0:T(4,128)S(1)}, f32[4,128]{1,0:T(4,128)}, u32[]{:S(2)}) copy-start(f32[4,128]{1,0:T(4,128)} %get-tuple-element.8) | copy-start | bytes 6148
